TPU v7x, 512 devices: a whole 4x8x8 slice. The times are simulated.
512 devices in a mesh: rep: 32 (over x, y_hi, core), chan: 16 (over y_lo, z).
Axes of the slice: x: 4, y: 8 (y_hi: 4, y_lo: 2; y = y_hi * 2 + y_lo), z: 8, core: 2. Of those that a mesh axis runs over, the one named last changes fastest.
Arguments:
- features: bfloat16 [32, 512, 1024], P('rep', 'chan'), may hold values from -6 to 6
- filters: bfloat16 [9, 512, 512], P(None, 'chan'), may hold values from -0.09375 to 0.09375
- cotangent: bfloat16 [32, 512, 1024], P('rep', 'chan'), may hold values from -6 to 6
Outputs:
- result_maps: bfloat16 [32, 512, 1024], P('rep', 'chan')
- input_grad: bfloat16 [32, 512, 1024], P('rep', 'chan')
- filter_grad: float32 [9, 512, 512], P(None, 'chan')
All inputs are finite; a program needn't handle non-finite values.
Results may differ from a plain program's by a relative error of at most 0.001.
Values may be sent and summed in bfloat16 or wider, within the bound.
A program may use at most 64 MiB of HBM per device.

v0:
```python
import jax
import jax.numpy as jnp
from jax import lax
from jax.sharding import PartitionSpec as P

MAP_W = 64


offsets = [(a, b) for a in (-1, 0, 1) for b in (-1, 0, 1)]


def shifted(value, row_step, col_step):
    cells = value.shape[-1]
    margin = MAP_W + 1
    padded = jnp.pad(value, [(0, 0)] * (value.ndim - 1) + [(margin, margin)])
    begin = margin + row_step * MAP_W + col_step
    taken = lax.slice_in_dim(padded, begin, begin + cells, axis=value.ndim - 1)
    column = jnp.arange(cells) % MAP_W + col_step
    keep = (column >= 0) & (column < MAP_W)
    return jnp.where(keep, taken, jnp.zeros_like(taken))


def per_device(features, filters, cotangent):
    local_taps = jnp.stack([shifted(features, a, b) for a, b in offsets])
    owned = lax.psum_scatter(
        jnp.einsum("tio,tsip->osp", filters, local_taps, preferred_element_type=jnp.float32),
        "chan",
        scatter_dimension=0,
        tiled=True,
    )
    result_maps = jnp.transpose(owned, (1, 0, 2)).astype(jnp.bfloat16)
    gathered = lax.all_gather(cotangent, "chan", axis=1, tiled=True)
    grad_terms = jnp.einsum(
        "tsip,sop->tio", local_taps, gathered, preferred_element_type=jnp.float32
    )
    samples_all = features.shape[0] * lax.axis_size("rep")
    filter_grad = lax.psum(grad_terms, "rep") / samples_all
    back_total = jnp.zeros(features.shape, jnp.float32)
    for index, (a, b) in enumerate(offsets):
        back_total = back_total + jnp.einsum(
            "io,sop->sip",
            filters[index],
            shifted(gathered, -a, -b),
            preferred_element_type=jnp.float32,
        )
    input_grad = back_total.astype(jnp.bfloat16)
    return (result_maps, input_grad, filter_grad)


def solution(mesh):
    return jax.shard_map(
        per_device,
        mesh=mesh,
        in_specs=(P("rep", "chan", None), P(None, "chan", None), P("rep", "chan", None)),
        out_specs=(P("rep", "chan", None), P("rep", "chan", None), P(None, "chan", None)),
        check_vma=False,
    )
```

profile of v0, /device:TPU:1, one launch (start us, length us, event | category | flops | bytes accessed | tf_op | source)
XLA Modules:
  0.0 693.0 jit_solution(4624190967968672387)
XLA Ops:
  7.2 0.0 all-gather.2.cloned.1.call-start
  7.2 0.7 all-gather.2.cloned.1.call-update
  7.9 0.0 all-reduce.6.cloned.1.call-start
  8.0 0.9 fusion.53
  8.9 0.9 fusion.56
  9.9 0.9 fusion.59
  10.8 0.9 fusion.62
  11.7 0.9 bitcast_dynamic-update-slice_fusion
  12.6 0.9 fusion.65
  13.5 0.9 fusion.68
  14.5 0.9 fusion.71
  15.4 0.9 fusion.74
  16.3 3.0 convolution_bitcast_fusion
  19.4 4.7 copy.32
  24.1 1.3 dynamic-slice
  26.0 377.3 %all-reduce.7 = bf16[512,1,1024]{2,1,0:T(2,128)(2,1)} all-reduce(f32[512,1,1024]{2,1,0:T(1,128)S(1)} %copy.32), channel_id=2, replica_groups=mesh['rep'=32,'chan'=16] {'chan'}, use_global_device_ids=true, to_apply=%region_0.1.clone | all-reduce | flops 524288 | bytes 3145728
  403.3 1.0 constant_dynamic-slice_fusion
  404.4 0.7 copy.37
  405.0 0.0 copy-start.1
  405.0 0.0 all-gather.2.cloned.1.call-done
  405.0 0.0 copy-start
  405.0 2.7 fusion.25
  407.7 0.0 all-reduce.6.cloned.1.call-update
  407.7 0.0 copy-done.1
  407.7 0.0 copy-done
  407.7 0.5 fusion.29
  408.2 0.5 convolution_add_fusion.7
  408.7 0.5 convolution_add_fusion.6
  409.2 0.5 convolution_add_fusion.5
  409.7 0.3 convolution_add_fusion.4
  410.0 0.5 convolution_add_fusion.3
  410.5 0.5 convolution_add_fusion.2
  411.0 0.5 convolution_add_fusion.1
  411.5 1.1 fusion.1
  412.6 271.7 %all-reduce.6.cloned.1.call-done = f32[9,32,512]{2,1,0:T(8,128)} async-done(((f32[9,32,512]{2,1,0:T(8,128)}), f32[9,32,512]{2,1,0:T(8,128)}) %all-reduce.6.cloned.1.call-update) | async-done | bytes 589840 | tf_op jit(solution)/shard_map/psum | solution.py:37
  684.3 1.9 broadcast_multiply_fusion
  (3 shorter events, 0.0 us)
Async XLA Ops:
  7.2 397.9 %all-gather.2.cloned.1.call-start = ((), (), s32[]{:S(2)}) async-start(), calls=%async_computation | async-start | bytes 1114112 | tf_op jit(solution)/shard_map/all_gather | solution.py:32
  7.9 676.4 %all-reduce.6.cloned.1.call-start = ((), (), s32[]{:S(2)}) async-start(), calls=%async_computation.1 | async-start | bytes 1179648 | tf_op jit(solution)/shard_map/psum | solution.py:37
  405.0 2.7 copy-start.1
  405.0 2.7 copy-start
Sparse Core Ops, SparseCore 0:
  10.1 72.7 all-gather.1
  407.8 276.3 all-reduce.5
where the time goes:
time: 695 us; the launch traced here: 693 us
  blocking collectives  377 us (54%)
  waiting for transfers between devices  272 us (39%)
  between operations  14.8 us (2%)
  matrix products  10.5 us (2%)
  other arithmetic  10.2 us (1%)
  local copies, waits for them, and re-layouts  7.71 us (1%)
    unnamed x1, blocking collectives  377 us
    psum x1, waiting for transfers between devices, per_device(): filter_grad = lax.psum(grad_terms, 'rep') / samples_all  272 us
  transfers between devices with their start and end apart: 2, of which 1 were waited for; matrix products, arithmetic and copies ran while one was open for 3% of the time, Pallas kernels for 0%

commit v1 on v0

v1 whole, which is shorter than its diff:
```python
import jax
import jax.numpy as jnp
from jax import lax
from jax.experimental import pallas as pl
from jax.experimental.pallas import tpu as pltpu
from jax.sharding import PartitionSpec as P

MESH = pl.DeviceIdType.MESH
F32 = jnp.float32
BF16 = jnp.bfloat16

CELLS = 1024
OFFSETS = [(a, b) for a in (-1, 0, 1) for b in (-1, 0, 1)]

STEPS = [
    [(0, 0, 0, 1, 0), (0, 0, 0, -1, 0), (0, 0, 1, 0, 0), (0, 0, 0, 2, 0), (0, 0, 0, -2, 0)],
    [(0, -1, 1, 0, 0), (0, 1, 1, 0, 0), (0, -2, 0, 1, 0), (0, 2, 0, -1, 0), (0, -2, 1, 0, 0), (0, 2, 1, 0, 0),
     (0, -2, 0, 2, 1), (0, 2, 0, -2, 2)],
    [(1, -2, 0, 1, 0), (1, 2, 0, -1, 0), (1, -2, 0, 2, 1), (1, 2, 0, -2, 2)],
]
COPIES = sum(len(s) for s in STEPS)
CHIPS = [(dx, dh) for dx in range(4) for dh in range(4) if (dx, dh) != (0, 0)]
PEERS = [(dy, dz) for dy in range(2) for dz in range(8) if (dy, dz) != (0, 0)]


def coords():
    rep = lax.axis_index("rep")
    chan = lax.axis_index("chan")
    return rep // 8, (rep // 2) % 4, rep % 2, chan // 8, chan % 8


def keep_mask(a, b):
    p = lax.broadcasted_iota(jnp.int32, (32, CELLS), 1)
    row = p // 64 + a
    col = p % 64 + b
    return (row >= 0) & (row < 16) & (col >= 0) & (col < 64)


def moved(value, a, b):
    step = 64 * a + b
    if step == 0:
        return value
    return jnp.where(keep_mask(a, b), pltpu.roll(value, (-step) % CELLS, 1), 0.0)


def kernel(feat, filt, cot, maps_out, igrad_out, fgrad_out,
           c_all, f_all, w_all, w_send, taps, prod, grad, pair, half, slots, mine, full,
           c_ss, c_rs, f_ss, f_rs, w_ss, w_rs, r_ss, r_rs, a_ss, a_rs, k_ss, k_rs):
    x, h, core, yl, z = coords()
    rep = lax.axis_index("rep")
    chan = lax.axis_index("chan")

    def chan_dev(dy, dz):
        return (rep, ((yl + dy) % 2) * 8 + (z + dz + 8) % 8)

    def chip_dev(dx, dh):
        return ((((x + dx) % 4) * 4 + (h + dh) % 4) * 2 + core, chan)

    sibling = ((x * 4 + h) * 2 + 1 - core, chan)

    barrier = pltpu.get_barrier_semaphore()
    for dev in [chan_dev(*d) for d in PEERS] + [chip_dev(*d) for d in CHIPS] + [sibling]:
        pl.semaphore_signal(barrier, inc=1, device_id=dev, device_id_type=MESH)

    own_rows = pl.ds(pl.multiple_of(chan * 32, 32), 32)
    c_all[own_rows, :] = cot[0]
    f_all[own_rows, :] = feat[0]
    pl.semaphore_wait(barrier, len(PEERS) + len(CHIPS) + 1)

    def cols(part):
        return [pl.ds(0, CELLS), pl.ds(0, CELLS // 2), pl.ds(CELLS // 2, CELLS // 2)][part]

    def gather(own, buf, ss, rs):
        def rows(dy, dz):
            owner = ((yl + dy) % 2) * 8 + (z + dz + 8) % 8
            return pl.ds(pl.multiple_of(owner * 32, 32), 32)

        def send_copy(n, item):
            dy, dz, hy, hz, part = item
            src = own.at[0, :, cols(part)] if (dy, dz) == (0, 0) else buf.at[rows(dy, dz), cols(part)]
            return pltpu.make_async_remote_copy(
                src_ref=src, dst_ref=buf.at[rows(dy, dz), cols(part)],
                send_sem=ss.at[n], recv_sem=rs.at[n],
                device_id=chan_dev(hy, hz), device_id_type=MESH)

        def recv_copy(n, item):
            dy, dz, hy, hz, part = item
            place = buf.at[rows(dy + hy, dz - hz), cols(part)]
            return pltpu.make_async_remote_copy(
                src_ref=place, dst_ref=place,
                send_sem=ss.at[n], recv_sem=rs.at[n],
                device_id=chan_dev(hy, hz), device_id_type=MESH)

        numbered, n = [], 0
        for step in STEPS:
            numbered.append([(n + k, item) for k, item in enumerate(step)])
            n += len(step)

        def send(s):
            for n, item in numbered[s]:
                send_copy(n, item).start()

        def recv(s):
            for n, item in numbered[s]:
                recv_copy(n, item).wait_recv()

        def drain():
            for step in numbered:
                for n, item in step:
                    send_copy(n, item).wait_send()

        return send, recv, drain

    c_send, c_recv, c_drain = gather(cot, c_all, c_ss, c_rs)
    f_send, f_recv, f_drain = gather(feat, f_all, f_ss, f_rs)

    c_send(0)

    value = feat[0].astype(F32)
    for t, (a, b) in enumerate(OFFSETS):
        taps[t * 32:(t + 1) * 32, :] = moved(value, a, b).astype(BF16)
    grad[9] = jnp.zeros((32, 512), F32)

    c_recv(0)
    c_send(1)

    for d in range(16):
        parts = [filt[t, :, d * 32:(d + 1) * 32].astype(F32) for t in range(9)]
        parts.append(jnp.zeros((32, 96), F32))
        w_send[d] = jnp.concatenate(parts, axis=1).astype(BF16)
    my_rows = pl.ds(pl.multiple_of(core * 16, 16), 16)
    their_rows = pl.ds(pl.multiple_of((1 - core) * 16, 16), 16)
    w_all[chan] = w_send[chan]

    c_recv(1)
    c_send(2)
    f_send(0)

    def w_copy(n, dy, dz):
        to = ((yl + dy) % 2) * 8 + (z + dz) % 8
        return pltpu.make_async_remote_copy(
            src_ref=w_send.at[to, my_rows], dst_ref=w_all.at[chan, my_rows],
            send_sem=w_ss.at[n], recv_sem=w_rs.at[n],
            device_id=chan_dev(dy, dz), device_id_type=MESH)

    def w_arrival(n, dy, dz):
        place = w_all.at[((yl + dy) % 2) * 8 + (z - dz + 8) % 8, my_rows]
        return pltpu.make_async_remote_copy(
            src_ref=place, dst_ref=place, send_sem=w_ss.at[n], recv_sem=w_rs.at[n],
            device_id=chan_dev(dy, dz), device_id_type=MESH)

    for n, (dy, dz) in enumerate(PEERS):
        w_copy(n, dy, dz).start()

    c_recv(2)

    def grad_tile(n, _):
        rows = pl.ds(pl.multiple_of(n * 256, 256), 256)
        tile = lax.dot_general(taps[...], c_all[rows, :], (((1,), (1,)), ((), ())), preferred_element_type=F32)
        grad[0:9, :, rows] = tile.reshape(9, 32, 256)
        return 0

    lax.fori_loop(0, 2, grad_tile, 0)

    def sib_copy(n, src, dst):
        return pltpu.make_async_remote_copy(
            src_ref=src, dst_ref=dst, send_sem=k_ss.at[n], recv_sem=k_rs.at[n],
            device_id=sibling, device_id_type=MESH)

    my_taps = pl.ds(core * 5, 5)
    other_taps = pl.ds((1 - core) * 5, 5)
    pair_copy = sib_copy(0, grad.at[other_taps], pair)
    pair_copy.start()

    f_recv(0)
    f_send(1)

    pair_copy.wait()
    half[...] = grad[my_taps] + pair[...]

    def place(dx, dh):
        return pl.ds(pl.multiple_of(((h + dh) % 4) * 8, 8), 8), pl.ds(pl.multiple_of(((x + dx) % 4) * 128, 128), 128)

    def rs_copy(n, dx, dh):
        r, c = place(dx, dh)
        return pltpu.make_async_remote_copy(
            src_ref=half.at[:, r, c], dst_ref=slots.at[n],
            send_sem=r_ss.at[n], recv_sem=r_rs.at[n],
            device_id=chip_dev(dx, dh), device_id_type=MESH)

    for n, d in enumerate(CHIPS):
        rs_copy(n, *d).start()

    def tap_products(lhs, rhs):
        def tile(n, _):
            c = pl.ds(pl.multiple_of(n * 256, 256), 256)
            prod[:, c] = lhs(rhs[:, c])
            return 0

        lax.fori_loop(0, 4, tile, 0)

    def tap_sum(sign):
        total = prod[4 * 32:5 * 32, :]
        for t, (a, b) in enumerate(OFFSETS):
            if t != 4:
                total = total + moved(prod[t * 32:(t + 1) * 32, :], sign * a, sign * b)
        return total

    tap_products(lambda v: jnp.dot(filt[...].reshape(288, 512), v, preferred_element_type=F32), c_all)
    igrad_out[0] = tap_sum(-1).astype(BF16)

    f_recv(1)
    f_send(2)

    r0, c0 = place(0, 0)
    for n, d in enumerate(CHIPS):
        rs_copy(n, *d).wait_recv()
    total = half[:, r0, c0]
    for n in range(15):
        total = total + slots[n]
    total = total * (1.0 / 32.0)
    mine[...] = total
    full[my_taps, r0, c0] = total

    def ag_copy(n, dx, dh):
        return pltpu.make_async_remote_copy(
            src_ref=mine, dst_ref=full.at[my_taps, r0, c0],
            send_sem=a_ss.at[n], recv_sem=a_rs.at[n],
            device_id=chip_dev(dx, dh), device_id_type=MESH)

    def ag_arrival(n, dx, dh):
        r, c = place(4 - dx, 4 - dh)
        spot = full.at[my_taps, r, c]
        return pltpu.make_async_remote_copy(
            src_ref=spot, dst_ref=spot, send_sem=a_ss.at[n], recv_sem=a_rs.at[n],
            device_id=chip_dev(dx, dh), device_id_type=MESH)

    for n, d in enumerate(CHIPS):
        ag_copy(n, *d).start()

    for n, d in enumerate(PEERS):
        w_arrival(n, *d).wait_recv()
    w_pair = sib_copy(1, w_all.at[:, my_rows], w_all.at[:, my_rows])
    w_pair_in = sib_copy(1, w_all.at[:, their_rows], w_all.at[:, their_rows])
    w_pair.start()
    f_recv(2)
    w_pair_in.wait_recv()

    def forward(v):
        return lax.dot_general(w_all[...].reshape(512, 384)[:, :288], v, (((0,), (0,)), ((), ())),
                               preferred_element_type=F32)

    tap_products(forward, f_all)
    maps_out[0] = tap_sum(1).astype(BF16)

    for n, d in enumerate(CHIPS):
        ag_arrival(n, *d).wait_recv()
    out_pair = sib_copy(2, full.at[my_taps], full.at[my_taps])
    out_pair_in = sib_copy(2, full.at[other_taps], full.at[other_taps])
    out_pair.start()
    out_pair_in.wait_recv()
    fgrad_out[...] = full[0:9]

    out_pair.wait_send()
    w_pair.wait_send()
    c_drain()
    f_drain()
    for n, d in enumerate(PEERS):
        w_copy(n, *d).wait_send()
    for n, d in enumerate(CHIPS):
        rs_copy(n, *d).wait_send()
        ag_copy(n, *d).wait_send()


def per_device(features, filters, cotangent):
    vmem = pl.BlockSpec(memory_space=pltpu.VMEM)
    dma = pltpu.SemaphoreType.DMA
    return tuple(pl.pallas_call(
        kernel,
        out_shape=(
            jax.ShapeDtypeStruct((1, 32, CELLS), BF16),
            jax.ShapeDtypeStruct((1, 32, CELLS), BF16),
            jax.ShapeDtypeStruct((9, 32, 512), F32),
        ),
        in_specs=[vmem] * 3,
        out_specs=(vmem,) * 3,
        scratch_shapes=[
            pltpu.VMEM((512, CELLS), BF16),
            pltpu.VMEM((512, CELLS), BF16),
            pltpu.VMEM((16, 32, 384), BF16),
            pltpu.VMEM((16, 32, 384), BF16),
            pltpu.VMEM((288, CELLS), BF16),
            pltpu.VMEM((288, CELLS), F32),
            pltpu.VMEM((10, 32, 512), F32),
            pltpu.VMEM((5, 32, 512), F32),
            pltpu.VMEM((5, 32, 512), F32),
            pltpu.VMEM((15, 5, 8, 128), F32),
            pltpu.VMEM((5, 8, 128), F32),
            pltpu.VMEM((10, 32, 512), F32),
            dma((COPIES,)), dma((COPIES,)), dma((COPIES,)), dma((COPIES,)),
            dma((15,)), dma((15,)), dma((15,)), dma((15,)), dma((15,)), dma((15,)),
            dma((3,)), dma((3,)),
        ],
        compiler_params=pltpu.CompilerParams(
            collective_id=0, has_side_effects=True, vmem_limit_bytes=32 * 1024 * 1024),
        cost_estimate=pl.CostEstimate(flops=906_000_000, bytes_accessed=1_200_000, transcendentals=0),
        name="conv",
    )(features, filters, cotangent))


def solution(mesh):
    return jax.shard_map(
        per_device,
        mesh=mesh,
        in_specs=(P("rep", "chan", None), P(None, "chan", None), P("rep", "chan", None)),
        out_specs=(P("rep", "chan", None), P("rep", "chan", None), P(None, "chan", None)),
        check_vma=False,
    )
```

time: 695 us -> 71.7 us (0.10)
  blocking collectives: 377 us -> 0 us
  waiting for transfers between devices: 272 us -> 0 us
  Pallas kernels: 0 us -> 66.1 us
  between operations: 14.8 us -> 0.65 us
  matrix products: 10.5 us -> 0 us
  other arithmetic: 10.2 us -> 0 us
    unnamed x1 -> x0, blocking collectives: 377 us -> none
    psum x1 -> x0, waiting for transfers between devices: 272 us -> none  [per_device(): filter_grad = lax.psum(grad_terms, 'rep') / samples_all]
    pallas_call x0 -> x1, Pallas kernels: none -> 66.1 us  [per_device(): pl.pallas_call(kernel, out_shape=(jax.ShapeDtypeStruct((1, 32, CELLS), BF...]
    dot_general x11 -> x0, matrix products: 10.5 us -> none  [the longest x9 4.85 us: per_device(): jnp.einsum('io,sop->sip', filters[index], shifted(gathered, -a, -b), pref...]
    unnamed x8 -> x0, other arithmetic: 7.36 us -> none
  transfers between devices with their start and end apart: 2 -> 0, of which waited for: 1 -> 0; matrix products, arithmetic and copies ran while one was open for 3% -> 0% of each run, Pallas kernels for 0% -> 0%
where the time goes in v1:
time: 71.7 us; the launch traced here: 71.4 us
  Pallas kernels  66.1 us (92%)
  local copies, waits for them, and re-layouts  4.71 us (7%)
    pallas_call x1, Pallas kernels, per_device(): pl.pallas_call(kernel, out_shape=(jax.ShapeDtypeStruct((1, 32, CELLS), BF...  66.1 us
    unnamed x9, local copies, waits for them, and re-layouts  4.71 us

profile of v1, /device:TPU:1, one launch (start us, length us, event | category | flops | bytes accessed | tf_op | source)
XLA Modules:
  0.0 71.4 jit_solution(3604079156516792151)
XLA Ops:
  0.6 0.0 copy-start
  0.6 1.0 %copy-done = bf16[9,32,512]{2,1,0:T(8,128)(2,1)S(1)} copy-done((bf16[9,32,512]{2,1,0:T(8,128)(2,1)S(1)}, bf16[9,32,512]{2,1,0:T(8,128)(2,1)}, u32[]{:S(2)}) %copy-start) | copy-done | bytes 294936
  1.6 0.0 copy-start.1
  1.6 0.8 %copy-done.1 = bf16[1,32,1024]{2,1,0:T(8,128)(2,1)S(1)} copy-done((bf16[1,32,1024]{2,1,0:T(8,128)(2,1)S(1)}, bf16[1,32,1024]{2,1,0:T(8,128)(2,1)}, u32[]{:S(2)}) %copy-start.1) | copy-done | bytes 65560
  2.4 0.0 copy-start.2
  2.4 0.8 %copy-done.2 = bf16[1,32,1024]{2,1,0:T(8,128)(2,1)S(1)} copy-done((bf16[1,32,1024]{2,1,0:T(8,128)(2,1)S(1)}, bf16[1,32,1024]{2,1,0:T(8,128)(2,1)}, u32[]{:S(2)}) %copy-start.2) | copy-done | bytes 65560
  3.3 66.1 %conv.1 = (bf16[1,32,1024]{2,1,0:T(8,128)(2,1)S(1)}, bf16[1,32,1024]{2,1,0:T(8,128)(2,1)S(1)}, f32[9,32,512]{2,1,0:T(8,128)S(1)}) custom-call(bf16[1,32,1024]{2,1,0:T(8,128)(2,1)S(1)} %copy-done.1, bf16[9,32,512]{2,1,0:T(8,128)(2,1)S(1)} %copy-done, bf16[1,32,1024]{2,1,0:T(8,128)(2,1)S(1)} %copy-done.2), custom_call_target="tpu_custom_call" | custom-call | flops 906000000 | bytes 1200000 | tf_op jit(solution)/shard_map/conv/pallas_call | solution.py:278
  69.4 0.6 copy.9
  70.0 0.6 copy.10
  70.6 0.8 %copy.11 = f32[9,32,512]{2,1,0:T(8,128)} copy(f32[9,32,512]{2,1,0:T(8,128)S(1)} %get-tuple-element.8) | data formatting | bytes 1179648
Async XLA Ops:
  0.6 1.0 %copy-start = (bf16[9,32,512]{2,1,0:T(8,128)(2,1)S(1)}, bf16[9,32,512]{2,1,0:T(8,128)(2,1)}, u32[]{:S(2)}) copy-start(bf16[9,32,512]{2,1,0:T(8,128)(2,1)} %filt.1) | copy-start | bytes 884740
  1.6 0.8 %copy-start.1 = (bf16[1,32,1024]{2,1,0:T(8,128)(2,1)S(1)}, bf16[1,32,1024]{2,1,0:T(8,128)(2,1)}, u32[]{:S(2)}) copy-start(bf16[1,32,1024]{2,1,0:T(8,128)(2,1)} %feat.1) | copy-start | bytes 196612
  2.4 0.8 %copy-start.2 = (bf16[1,32,1024]{2,1,0:T(8,128)(2,1)S(1)}, bf16[1,32,1024]{2,1,0:T(8,128)(2,1)}, u32[]{:S(2)}) copy-start(bf16[1,32,1024]{2,1,0:T(8,128)(2,1)} %cot.1) | copy-start | bytes 196612

commit v2 on v0

v2 whole, which is shorter than its diff:
```python
import jax
import jax.numpy as jnp
from jax import lax
from jax.experimental import pallas as pl
from jax.experimental.pallas import tpu as pltpu
from jax.sharding import PartitionSpec as P

MESH = pl.DeviceIdType.MESH
F32 = jnp.float32
BF16 = jnp.bfloat16

CELLS = 1024
OFFSETS = [(a, b) for a in (-1, 0, 1) for b in (-1, 0, 1)]
CHIPS = [(dx, dh) for dx in range(4) for dh in range(4) if (dx, dh) != (0, 0)]
PEERS = [(dy, dz) for dy in range(2) for dz in range(8) if (dy, dz) != (0, 0)]
NSEM = 96


def coords():
    rep = lax.axis_index("rep")
    chan = lax.axis_index("chan")
    return rep // 8, (rep // 2) % 4, rep % 2, chan // 8, chan % 8


def keep_mask(a, b):
    p = lax.broadcasted_iota(jnp.int32, (32, CELLS), 1)
    row = p // 64 + a
    col = p % 64 + b
    return (row >= 0) & (row < 16) & (col >= 0) & (col < 64)


def moved(value, a, b):
    step = 64 * a + b
    if step == 0:
        return value
    return jnp.where(keep_mask(a, b), pltpu.roll(value, (-step) % CELLS, 1), 0.0)


def kernel(feat_in, filt_in, cot_in, maps_out, igrad_out, fgrad_out,
           filt, c_all, f_all, w_all, w_send, taps, prod, grad, pair, half, slots, mine, full,
           in_sem, ss, rs, r_ss, r_rs):
    x, h, core, yl, z = coords()
    rep = lax.axis_index("rep")
    chan = lax.axis_index("chan")

    def chan_of(dy, dz):
        return ((yl + dy) % 2) * 8 + (z + dz + 8) % 8

    def chan_dev(dy, dz):
        return (rep, chan_of(dy, dz))

    def chip_dev(dx, dh):
        return ((((x + dx) % 4) * 4 + (h + dh) % 4) * 2 + core, chan)

    sibling = ((x * 4 + h) * 2 + 1 - core, chan)

    def rows(dy, dz):
        return pl.ds(pl.multiple_of(chan_of(dy, dz) * 32, 32), 32)

    barrier = pltpu.get_barrier_semaphore()
    for dev in [chan_dev(*d) for d in PEERS] + [chip_dev(*d) for d in CHIPS] + [sibling]:
        pl.semaphore_signal(barrier, inc=1, device_id=dev, device_id_type=MESH)

    loads = [
        pltpu.make_async_copy(cot_in.at[0], c_all.at[rows(0, 0)], in_sem.at[0]),
        pltpu.make_async_copy(feat_in.at[0], f_all.at[rows(0, 0)], in_sem.at[1]),
        pltpu.make_async_copy(filt_in, filt, in_sem.at[2]),
    ]
    for load in loads:
        load.start()
    for load in loads:
        load.wait()
    pl.semaphore_wait(barrier, len(PEERS) + len(CHIPS) + 1)

    sends, pending = [], {}

    def start(key, src, dst, arrival, dev):
        n = len(sends)
        copy = pltpu.make_async_remote_copy(
            src_ref=src, dst_ref=dst, send_sem=ss.at[n], recv_sem=rs.at[n], device_id=dev, device_id_type=MESH)
        copy.start()
        sends.append(copy)
        pending[key] = pltpu.make_async_remote_copy(
            src_ref=arrival, dst_ref=arrival, send_sem=ss.at[n], recv_sem=rs.at[n], device_id=dev, device_id_type=MESH)

    def arrive(key):
        pending.pop(key).wait_recv()

    def pass_on(name, buf, dy, dz, hy, hz, part=0):
        cols = [pl.ds(0, CELLS), pl.ds(0, CELLS // 2), pl.ds(CELLS // 2, CELLS // 2)][part]
        place = buf.at[rows(dy, dz), cols]
        start((name, (dy + hy) % 2, dz - hz, part), place, place, buf.at[rows(dy + hy, dz - hz), cols], chan_dev(hy, hz))

    pass_on("c", c_all, 0, 0, 1, 0)
    for dz in (1, -1, 2, -2, 3, -3):
        pass_on("c", c_all, 0, 0, 0, dz)
    pass_on("f", f_all, 0, 0, 1, 0)

    value = f_all[rows(0, 0), :].astype(F32)
    for t, (a, b) in enumerate(OFFSETS):
        taps[t * 32:(t + 1) * 32, :] = moved(value, a, b).astype(BF16)
    grad[9] = jnp.zeros((32, 512), F32)

    for dz in (1, -1, 2, -2):
        arrive(("c", 0, dz, 0))
        pass_on("c", c_all, 0, dz, 1, 0)
    for dz in (3, -3):
        arrive(("c", 0, dz, 0))
        if dz == 3:
            pass_on("c", c_all, 0, 3, 0, -1, 1)
        else:
            pass_on("c", c_all, 0, -3, 0, 1, 2)
        pass_on("c", c_all, 0, dz, 1, 0)

    arrive(("f", 1, 0, 0))
    for dz in (1, -1, 2, -2, 3, -3):
        for dy in (0, 1):
            pass_on("f", f_all, dy, 0, 0, dz)

    for d in range(16):
        parts = [filt[t, :, d * 32:(d + 1) * 32].astype(F32) for t in range(9)]
        parts.append(jnp.zeros((32, 96), F32))
        w_send[d] = jnp.concatenate(parts, axis=1).astype(BF16)
    my_rows = pl.ds(pl.multiple_of(core * 16, 16), 16)
    their_rows = pl.ds(pl.multiple_of((1 - core) * 16, 16), 16)
    w_all[chan] = w_send[chan]

    arrive(("c", 0, 4, 1))
    pass_on("c", c_all, 0, 4, 1, 0, 1)
    arrive(("c", 0, -4, 2))
    pass_on("c", c_all, 0, -4, 1, 0, 2)

    my_taps = pl.ds(core * 5, 5)
    other_taps = pl.ds((1 - core) * 5, 5)

    def place(lane_tile, dh):
        return pl.ds(pl.multiple_of(((h + dh) % 4) * 8, 8), 8), pl.ds(pl.multiple_of(lane_tile * 128, 128), 128)

    def column(dy):
        return pl.ds(pl.multiple_of(((yl + dy) % 2) * 256, 256), 256)

    def grad_column(dy):
        side = column(dy)
        tile = lax.dot_general(taps[...], c_all[side, :], (((1,), (1,)), ((), ())), preferred_element_type=F32)
        grad[0:9, :, side] = tile.reshape(9, 32, 256)
        start(("pair", dy), grad.at[other_taps, :, side], pair.at[:, :, side], pair.at[:, :, side], sibling)

    def reduce_copy(n, lane_tile, dh):
        r, c = place(lane_tile, dh)
        return pltpu.make_async_remote_copy(
            src_ref=half.at[:, r, c], dst_ref=slots.at[n], send_sem=r_ss.at[n], recv_sem=r_rs.at[n],
            device_id=((lane_tile * 4 + (h + dh) % 4) * 2 + core, chan), device_id_type=MESH)

    def reduce_column(dy):
        side = column(dy)
        arrive(("pair", dy))
        half[:, :, side] = grad[my_taps, :, side] + pair[:, :, side]
        for k in (0, 1):
            lane_tile = ((yl + dy) % 2) * 2 + k
            for dh in range(4):
                n = ((lane_tile - x + 4) % 4) * 4 + dh

                @pl.when(n != 0)
                def _():
                    reduce_copy(n, lane_tile, dh).start()

    grad_column(0)
    reduce_column(0)

    for n, (dy, dz) in enumerate(PEERS):
        start(("w", n), w_send.at[chan_of(dy, dz), my_rows], w_all.at[chan, my_rows],
              w_all.at[chan_of(dy, -dz), my_rows], chan_dev(dy, dz))

    for dz in (0, 1, -1, 2, -2, 3, -3):
        arrive(("c", 1, dz, 0))
    arrive(("c", 1, 4, 1))
    arrive(("c", 1, -4, 2))
    grad_column(1)
    reduce_column(1)

    def tap_products(lhs, rhs):
        def tile(n, _):
            c = pl.ds(pl.multiple_of(n * 256, 256), 256)
            prod[:, c] = lhs(rhs[:, c])
            return 0

        lax.fori_loop(0, 4, tile, 0)

    def tap_sum(sign):
        total = prod[4 * 32:5 * 32, :]
        for t, (a, b) in enumerate(OFFSETS):
            if t != 4:
                total = total + moved(prod[t * 32:(t + 1) * 32, :], sign * a, sign * b)
        return total

    tap_products(lambda v: jnp.dot(filt[...].reshape(288, 512), v, preferred_element_type=F32), c_all)
    igrad_out[0] = tap_sum(-1).astype(BF16)

    r0, c0 = place(x, 0)
    for n in range(1, 16):
        reduce_copy(n, x, 0).wait_recv()
    total = half[:, r0, c0]
    for n in range(1, 16):
        total = total + slots[n]
    total = total * (1.0 / 32.0)
    mine[...] = total
    full[my_taps, r0, c0] = total
    for dx, dh in CHIPS:
        r, c = place((x + 4 - dx) % 4, 4 - dh)
        start(("a", dx, dh), mine, full.at[my_taps, r0, c0], full.at[my_taps, r, c], chip_dev(dx, dh))

    def to_sibling(dx, dh):
        r, c = place((x + 4 - dx) % 4, 4 - dh)
        start(("o", dx, dh), full.at[my_taps, r, c], full.at[my_taps, r, c], full.at[other_taps, r, c], sibling)

    to_sibling(0, 0)

    for dy in (0, 1):
        arrive(("f", dy, 3, 0))
        pass_on("f", f_all, dy, 3, 0, -1, 1)
        arrive(("f", dy, -3, 0))
        pass_on("f", f_all, dy, -3, 0, 1, 2)

    for n, d in enumerate(PEERS):
        arrive(("w", n))
    start("wpair", w_all.at[:, my_rows], w_all.at[:, my_rows], w_all.at[:, their_rows], sibling)
    for dy in (0, 1):
        for dz in (1, -1, 2, -2):
            arrive(("f", dy, dz, 0))
        arrive(("f", dy, 4, 1))
        arrive(("f", dy, -4, 2))
    arrive("wpair")

    def forward(v):
        return lax.dot_general(w_all[...].reshape(512, 384)[:, :288], v, (((0,), (0,)), ((), ())),
                               preferred_element_type=F32)

    tap_products(forward, f_all)
    maps_out[0] = tap_sum(1).astype(BF16)

    for d in CHIPS:
        arrive(("a", *d))
        to_sibling(*d)
    arrive(("o", 0, 0))
    for d in CHIPS:
        arrive(("o", *d))
    fgrad_out[...] = full[0:9]

    for n in range(1, 16):
        reduce_copy(n, x, 0).wait_send()
    for copy in sends:
        copy.wait_send()
    assert not pending and len(sends) <= NSEM


def write_out(maps, igrad, fgrad, maps_out, igrad_out, fgrad_out, sem):
    copies = [
        pltpu.make_async_copy(fgrad, fgrad_out, sem.at[2]),
        pltpu.make_async_copy(maps, maps_out, sem.at[0]),
        pltpu.make_async_copy(igrad, igrad_out, sem.at[1]),
    ]
    for copy in copies:
        copy.start()
    for copy in copies:
        copy.wait()


def per_device(features, filters, cotangent):
    vmem = pl.BlockSpec(memory_space=pltpu.VMEM)
    hbm = pl.BlockSpec(memory_space=pltpu.HBM)
    dma = pltpu.SemaphoreType.DMA
    outs = (
        jax.ShapeDtypeStruct((1, 32, CELLS), BF16),
        jax.ShapeDtypeStruct((1, 32, CELLS), BF16),
        jax.ShapeDtypeStruct((9, 32, 512), F32),
    )
    features, filters, cotangent = (
        pltpu.with_memory_space_constraint(v, pltpu.HBM) for v in (features, filters, cotangent))
    results = pl.pallas_call(
        kernel,
        out_shape=outs,
        in_specs=[hbm] * 3,
        out_specs=(vmem,) * 3,
        scratch_shapes=[
            pltpu.VMEM((9, 32, 512), BF16),
            pltpu.VMEM((512, CELLS), BF16),
            pltpu.VMEM((512, CELLS), BF16),
            pltpu.VMEM((16, 32, 384), BF16),
            pltpu.VMEM((16, 32, 384), BF16),
            pltpu.VMEM((288, CELLS), BF16),
            pltpu.VMEM((288, CELLS), F32),
            pltpu.VMEM((10, 32, 512), F32),
            pltpu.VMEM((5, 32, 512), F32),
            pltpu.VMEM((5, 32, 512), F32),
            pltpu.VMEM((16, 5, 8, 128), F32),
            pltpu.VMEM((5, 8, 128), F32),
            pltpu.VMEM((10, 32, 512), F32),
            dma((3,)), dma((NSEM,)), dma((NSEM,)), dma((16,)), dma((16,)),
        ],
        compiler_params=pltpu.CompilerParams(
            collective_id=0, has_side_effects=True, vmem_limit_bytes=48 * 1024 * 1024),
        cost_estimate=pl.CostEstimate(flops=906_000_000, bytes_accessed=1_200_000, transcendentals=0),
        name="conv",
    )(features, filters, cotangent)
    return tuple(pl.pallas_call(
        write_out,
        out_shape=outs,
        in_specs=[pl.BlockSpec(memory_space=pl.ANY)] * 3,
        out_specs=(hbm,) * 3,
        compiler_params=pltpu.CompilerParams(vmem_limit_bytes=1024 * 1024),
        scratch_shapes=[dma((3,))],
        name="write_out",
    )(*results))


def solution(mesh):
    return jax.shard_map(
        per_device,
        mesh=mesh,
        in_specs=(P("rep", "chan", None), P(None, "chan", None), P("rep", "chan", None)),
        out_specs=(P("rep", "chan", None), P("rep", "chan", None), P(None, "chan", None)),
        check_vma=False,
    )
```

time: 695 us -> 61.7 us (0.09)
  blocking collectives: 377 us -> 0 us
  waiting for transfers between devices: 272 us -> 0 us
  Pallas kernels: 0 us -> 60.9 us
  between operations: 14.8 us -> 0.64 us
  matrix products: 10.5 us -> 0 us
  other arithmetic: 10.2 us -> 0 us
  local copies, waits for them, and re-layouts: 7.71 us -> 0 us
    unnamed x1 -> x0, blocking collectives: 377 us -> none
    psum x1 -> x0, waiting for transfers between devices: 272 us -> none  [per_device(): filter_grad = lax.psum(grad_terms, 'rep') / samples_all]
    pallas_call x0 -> x2, Pallas kernels: none -> 60.9 us  [the longest x1 60 us: per_device(): pl.pallas_call(kernel, out_shape=outs, in_specs=[hbm] * 3, out_specs=(vme...]
    dot_general x11 -> x0, matrix products: 10.5 us -> none  [the longest x9 4.85 us: per_device(): jnp.einsum('io,sop->sip', filters[index], shifted(gathered, -a, -b), pref...]
    unnamed x8 -> x0, other arithmetic: 7.36 us -> none
  transfers between devices with their start and end apart: 2 -> 0, of which waited for: 1 -> 0; matrix products, arithmetic and copies ran while one was open for 3% -> 0% of each run, Pallas kernels for 0% -> 0%
where the time goes in v2:
time: 61.7 us; the launch traced here: 61.5 us
  Pallas kernels  60.9 us (99%)
  between operations  0.64 us (1%)
    pallas_call x1, Pallas kernels, per_device(): pl.pallas_call(kernel, out_shape=outs, in_specs=[hbm] * 3, out_specs=(vme...  60 us

profile of v2, /device:TPU:1, one launch (start us, length us, event | category | flops | bytes accessed | tf_op | source)
XLA Modules:
  0.0 61.5 jit_solution(2562598565234922478)
XLA Ops:
  0.6 60.0 %conv.1 = (bf16[1,32,1024]{2,1,0:T(8,128)(2,1)S(1)}, bf16[1,32,1024]{2,1,0:T(8,128)(2,1)S(1)}, f32[9,32,512]{2,1,0:T(8,128)S(1)}) custom-call(bf16[1,32,1024]{2,1,0:T(8,128)(2,1)} %feat_in.1, bf16[9,32,512]{2,1,0:T(8,128)(2,1)} %filt_in.1, bf16[1,32,1024]{2,1,0:T(8,128)(2,1)} %cot_in.1), custom_call_target="tpu_custom_call" | custom-call | flops 906000000 | bytes 1200000 | tf_op jit(solution)/shard_map/conv/pallas_call | solution.py:279
  60.7 0.9 %write_out.1 = (bf16[1,32,1024]{2,1,0:T(8,128)(2,1)}, bf16[1,32,1024]{2,1,0:T(8,128)(2,1)}, f32[9,32,512]{2,1,0:T(8,128)}) custom-call(bf16[1,32,1024]{2,1,0:T(8,128)(2,1)S(1)} %get-tuple-element.6.maps, bf16[1,32,1024]{2,1,0:T(8,128)(2,1)S(1)} %get-tuple-element.7.igrad, f32[9,32,512]{2,1,0:T(8,128)S(1)} %get-tuple-element.8.fgrad), custom_call_target="tpu_custom_call" | custom-call | tf_op jit(solution)/shard_map/write_out/pallas_call | solution.py:305

commit v3 on v2

--- a/solution.py
+++ b/solution.py
@@ -11,7 +11,7 @@
 
 CELLS = 1024
 OFFSETS = [(a, b) for a in (-1, 0, 1) for b in (-1, 0, 1)]
-CHIPS = [(dx, dh) for dx in range(4) for dh in range(4) if (dx, dh) != (0, 0)]
+CHIPS = sorted([(dx, dh) for dx in range(4) for dh in range(4) if (dx, dh) != (0, 0)], key=lambda d: -(d[0] % 2 + 2 * (d[0] == 2) + 2 * (d[1] % 2) + 4 * (d[1] == 2)))
 PEERS = [(dy, dz) for dy in range(2) for dz in range(8) if (dy, dz) != (0, 0)]
 NSEM = 96
 
@@ -92,7 +92,7 @@
         start((name, (dy + hy) % 2, dz - hz, part), place, place, buf.at[rows(dy + hy, dz - hz), cols], chan_dev(hy, hz))
 
     pass_on("c", c_all, 0, 0, 1, 0)
-    for dz in (1, -1, 2, -2, 3, -3):
+    for dz in (2, -2, 1, -1):
         pass_on("c", c_all, 0, 0, 0, dz)
     pass_on("f", f_all, 0, 0, 1, 0)
 
@@ -101,15 +101,15 @@
         taps[t * 32:(t + 1) * 32, :] = moved(value, a, b).astype(BF16)
     grad[9] = jnp.zeros((32, 512), F32)
 
-    for dz in (1, -1, 2, -2):
+    for dz, side in ((2, 1), (-2, 2)):
         arrive(("c", 0, dz, 0))
-        pass_on("c", c_all, 0, dz, 1, 0)
-    for dz in (3, -3):
+        hop = -1 if dz > 0 else 1
+        pass_on("c", c_all, 0, dz, 0, hop)
+        pass_on("c", c_all, 0, dz, 0, 2 * hop, side)
+    pass_on("c", c_all, 0, 2, 1, 0)
+    pass_on("c", c_all, 0, -2, 1, 0)
+    for dz in (1, -1):
         arrive(("c", 0, dz, 0))
-        if dz == 3:
-            pass_on("c", c_all, 0, 3, 0, -1, 1)
-        else:
-            pass_on("c", c_all, 0, -3, 0, 1, 2)
         pass_on("c", c_all, 0, dz, 1, 0)
 
     arrive(("f", 1, 0, 0))
@@ -125,6 +125,9 @@
     their_rows = pl.ds(pl.multiple_of((1 - core) * 16, 16), 16)
     w_all[chan] = w_send[chan]
 
+    for dz in (3, -3):
+        arrive(("c", 0, dz, 0))
+        pass_on("c", c_all, 0, dz, 1, 0)
     arrive(("c", 0, 4, 1))
     pass_on("c", c_all, 0, 4, 1, 0, 1)
     arrive(("c", 0, -4, 2))
@@ -157,7 +160,7 @@
         half[:, :, side] = grad[my_taps, :, side] + pair[:, :, side]
         for k in (0, 1):
             lane_tile = ((yl + dy) % 2) * 2 + k
-            for dh in range(4):
+            for dh in (2, 1, 3, 0):
                 n = ((lane_tile - x + 4) % 4) * 4 + dh
 
                 @pl.when(n != 0)
@@ -166,10 +169,6 @@
 
     grad_column(0)
     reduce_column(0)
-
-    for n, (dy, dz) in enumerate(PEERS):
-        start(("w", n), w_send.at[chan_of(dy, dz), my_rows], w_all.at[chan, my_rows],
-              w_all.at[chan_of(dy, -dz), my_rows], chan_dev(dy, dz))
 
     for dz in (0, 1, -1, 2, -2, 3, -3):
         arrive(("c", 1, dz, 0))
@@ -177,6 +176,11 @@
     arrive(("c", 1, -4, 2))
     grad_column(1)
     reduce_column(1)
+
+    for n, (dy, dz) in enumerate(PEERS):
+        start(("w", n), w_send.at[chan_of(dy, dz), my_rows], w_all.at[chan, my_rows],
+              w_all.at[chan_of(dy, -dz), my_rows], chan_dev(dy, dz))
+
 
     def tap_products(lhs, rhs):
         def tile(n, _):
@@ -224,6 +228,9 @@
     for n, d in enumerate(PEERS):
         arrive(("w", n))
     start("wpair", w_all.at[:, my_rows], w_all.at[:, my_rows], w_all.at[:, their_rows], sibling)
+    for d in CHIPS:
+        arrive(("a", *d))
+        to_sibling(*d)
     for dy in (0, 1):
         for dz in (1, -1, 2, -2):
             arrive(("f", dy, dz, 0))
@@ -238,9 +245,6 @@
     tap_products(forward, f_all)
     maps_out[0] = tap_sum(1).astype(BF16)
 
-    for d in CHIPS:
-        arrive(("a", *d))
-        to_sibling(*d)
     arrive(("o", 0, 0))
     for d in CHIPS:
         arrive(("o", *d))

time: 61.7 us -> 56.4 us (0.914)
  Pallas kernels: 60.9 us -> 55.6 us
    pallas_call x1, Pallas kernels: 60 us -> 54.8 us  [per_device(): pl.pallas_call(kernel, out_shape=outs, in_specs=[hbm] * 3, out_specs=(vme...]
where the time goes in v3:
time: 56.4 us; the launch traced here: 56.3 us
  Pallas kernels  55.6 us (99%)
  between operations  0.64 us (1%)
    pallas_call x1, Pallas kernels, per_device(): pl.pallas_call(kernel, out_shape=outs, in_specs=[hbm] * 3, out_specs=(vme...  54.8 us

profile of v3, /device:TPU:1, one launch (start us, length us, event | category | flops | bytes accessed | tf_op | source)
XLA Modules:
  0.0 56.3 jit_solution(8194151111616859512)
XLA Ops:
  0.6 54.8 %conv.1 = (bf16[1,32,1024]{2,1,0:T(8,128)(2,1)S(1)}, bf16[1,32,1024]{2,1,0:T(8,128)(2,1)S(1)}, f32[9,32,512]{2,1,0:T(8,128)S(1)}) custom-call(bf16[1,32,1024]{2,1,0:T(8,128)(2,1)} %feat_in.1, bf16[9,32,512]{2,1,0:T(8,128)(2,1)} %filt_in.1, bf16[1,32,1024]{2,1,0:T(8,128)(2,1)} %cot_in.1), custom_call_target="tpu_custom_call" | custom-call | flops 906000000 | bytes 1200000 | tf_op jit(solution)/shard_map/conv/pallas_call | solution.py:283
  55.4 0.9 %write_out.1 = (bf16[1,32,1024]{2,1,0:T(8,128)(2,1)}, bf16[1,32,1024]{2,1,0:T(8,128)(2,1)}, f32[9,32,512]{2,1,0:T(8,128)}) custom-call(bf16[1,32,1024]{2,1,0:T(8,128)(2,1)S(1)} %get-tuple-element.6.maps, bf16[1,32,1024]{2,1,0:T(8,128)(2,1)S(1)} %get-tuple-element.7.igrad, f32[9,32,512]{2,1,0:T(8,128)S(1)} %get-tuple-element.8.fgrad), custom_call_target="tpu_custom_call" | custom-call | tf_op jit(solution)/shard_map/write_out/pallas_call | solution.py:309

commit v4 on v3

--- a/solution.py
+++ b/solution.py
@@ -36,8 +36,8 @@
     return jnp.where(keep_mask(a, b), pltpu.roll(value, (-step) % CELLS, 1), 0.0)
 
 
-def kernel(feat_in, filt_in, cot_in, maps_out, igrad_out, fgrad_out,
-           filt, c_all, f_all, w_all, w_send, taps, prod, grad, pair, half, slots, mine, full,
+def kernel(feat_in, filt_in, cot_in, maps_out, igrad_out, full,
+           filt, c_all, f_all, w_all, w_send, taps, prod, grad, pair, half, slots, mine,
            in_sem, ss, rs, r_ss, r_rs):
     x, h, core, yl, z = coords()
     rep = lax.axis_index("rep")
@@ -56,10 +56,6 @@
 
     def rows(dy, dz):
         return pl.ds(pl.multiple_of(chan_of(dy, dz) * 32, 32), 32)
-
-    barrier = pltpu.get_barrier_semaphore()
-    for dev in [chan_dev(*d) for d in PEERS] + [chip_dev(*d) for d in CHIPS] + [sibling]:
-        pl.semaphore_signal(barrier, inc=1, device_id=dev, device_id_type=MESH)
 
     loads = [
         pltpu.make_async_copy(cot_in.at[0], c_all.at[rows(0, 0)], in_sem.at[0]),
@@ -68,8 +64,12 @@
     ]
     for load in loads:
         load.start()
-    for load in loads:
-        load.wait()
+
+    barrier = pltpu.get_barrier_semaphore()
+    for dev in [chip_dev(*d) for d in CHIPS] + [chan_dev(*d) for d in PEERS] + [sibling]:
+        pl.semaphore_signal(barrier, inc=1, device_id=dev, device_id_type=MESH)
+
+    loads[0].wait()
     pl.semaphore_wait(barrier, len(PEERS) + len(CHIPS) + 1)
 
     sends, pending = [], {}
@@ -94,7 +94,9 @@
     pass_on("c", c_all, 0, 0, 1, 0)
     for dz in (2, -2, 1, -1):
         pass_on("c", c_all, 0, 0, 0, dz)
+    loads[1].wait()
     pass_on("f", f_all, 0, 0, 1, 0)
+    loads[2].wait()
 
     value = f_all[rows(0, 0), :].astype(F32)
     for t, (a, b) in enumerate(OFFSETS):
@@ -248,7 +250,6 @@
     arrive(("o", 0, 0))
     for d in CHIPS:
         arrive(("o", *d))
-    fgrad_out[...] = full[0:9]
 
     for n in range(1, 16):
         reduce_copy(n, x, 0).wait_send()
@@ -259,7 +260,7 @@
 
 def write_out(maps, igrad, fgrad, maps_out, igrad_out, fgrad_out, sem):
     copies = [
-        pltpu.make_async_copy(fgrad, fgrad_out, sem.at[2]),
+        pltpu.make_async_copy(fgrad.at[0:9], fgrad_out, sem.at[2]),
         pltpu.make_async_copy(maps, maps_out, sem.at[0]),
         pltpu.make_async_copy(igrad, igrad_out, sem.at[1]),
     ]
@@ -282,7 +283,7 @@
         pltpu.with_memory_space_constraint(v, pltpu.HBM) for v in (features, filters, cotangent))
     results = pl.pallas_call(
         kernel,
-        out_shape=outs,
+        out_shape=outs[:2] + (jax.ShapeDtypeStruct((10, 32, 512), F32),),
         in_specs=[hbm] * 3,
         out_specs=(vmem,) * 3,
         scratch_shapes=[
@@ -298,7 +299,6 @@
             pltpu.VMEM((5, 32, 512), F32),
             pltpu.VMEM((16, 5, 8, 128), F32),
             pltpu.VMEM((5, 8, 128), F32),
-            pltpu.VMEM((10, 32, 512), F32),
             dma((3,)), dma((NSEM,)), dma((NSEM,)), dma((16,)), dma((16,)),
         ],
         compiler_params=pltpu.CompilerParams(

time: 56.4 us -> 56.3 us (level)
  no operation moved by 1% of the time
where the time goes in v4:
time: 56.3 us; the launch traced here: 56.2 us
  Pallas kernels  55.6 us (99%)
  between operations  0.64 us (1%)
    pallas_call x1, Pallas kernels, per_device(): pl.pallas_call(kernel, out_shape=outs[:2] + (jax.ShapeDtypeStruct((10, 32...  54.7 us

profile of v4, /device:TPU:1, one launch (start us, length us, event | category | flops | bytes accessed | tf_op | source)
XLA Modules:
  0.0 56.2 jit_solution(16349102911917926169)
XLA Ops:
  0.6 54.7 %conv.1 = (bf16[1,32,1024]{2,1,0:T(8,128)(2,1)S(1)}, bf16[1,32,1024]{2,1,0:T(8,128)(2,1)S(1)}, f32[10,32,512]{2,1,0:T(8,128)S(1)}) custom-call(bf16[1,32,1024]{2,1,0:T(8,128)(2,1)} %feat_in.1, bf16[9,32,512]{2,1,0:T(8,128)(2,1)} %filt_in.1, bf16[1,32,1024]{2,1,0:T(8,128)(2,1)} %cot_in.1), custom_call_target="tpu_custom_call" | custom-call | flops 906000000 | bytes 1200000 | tf_op jit(solution)/shard_map/conv/pallas_call | solution.py:284
  55.3 0.9 %write_out.1 = (bf16[1,32,1024]{2,1,0:T(8,128)(2,1)}, bf16[1,32,1024]{2,1,0:T(8,128)(2,1)}, f32[9,32,512]{2,1,0:T(8,128)}) custom-call(bf16[1,32,1024]{2,1,0:T(8,128)(2,1)S(1)} %get-tuple-element.6.maps, bf16[1,32,1024]{2,1,0:T(8,128)(2,1)S(1)} %get-tuple-element.7.igrad, f32[10,32,512]{2,1,0:T(8,128)S(1)} %get-tuple-element.8.fgrad), custom_call_target="tpu_custom_call" | custom-call | tf_op jit(solution)/shard_map/write_out/pallas_call | solution.py:309
